TPU v7x, 32 devices: a whole 2x2x4 slice. The times are simulated.
32 devices in a mesh: groups: 2 (over x), node: 16 (over z, y, core).
Axes of the slice: x: 2, y: 2, z: 4, core: 2. Of those that a mesh axis runs over, the one named last changes fastest.
Arguments:
- unit_costs: bfloat16 [1024, 24, 2048], P(('groups', 'node')), parts along dimension 0, may hold values from -15 to 15
- hour_duals: bfloat16 [1024, 24, 2048], P(('groups', 'node')), parts along dimension 0, may hold values from -3 to 3
- inverse: bfloat16 [2048, 2048], replicated, may hold values from -0.5 to 1.5, as said below
- weights: int32 [1024], P(('groups', 'node')), parts along dimension 0, may hold values from 1 to 120
- section_three: int32 [1024], P(('groups', 'node')), parts along dimension 0, may hold values from 0 to 63, as said below
- prev_first: bfloat16 [16, 2048], P('groups'), parts along dimension 0, may hold values from -6 to 6
- prev_second: bfloat16 [32, 8, 512], P(('groups', 'node')), parts along dimension 0, may hold values from -6 to 6
- prev_third: bfloat16 [128, 8, 2048], P(('groups', 'node')), parts along dimension 0, may hold values from -6 to 6
- eta_mean: float32 [2], P('groups'), parts along dimension 0, may hold values from -2 to -1
- eta_duals: float32 [1024], P(('groups', 'node')), parts along dimension 0, may hold values from -1.2 to 1.2
Outputs:
- duals_new: bfloat16 [1024, 24, 2048], P(('groups', 'node')), parts along dimension 0
- first_avg: float32 [16, 2048], P('groups'), parts along dimension 0
- second_avg: float32 [32, 8, 512], P(('groups', 'node')), parts along dimension 0
- third_avg: float32 [128, 8, 2048], P(('groups', 'node')), parts along dimension 0
- eta_avg: float32 [2], P('groups'), parts along dimension 0
- eta_duals_new: float32 [1024], P(('groups', 'node')), parts along dimension 0
There are 2 independent parts, one for each index of `groups`. A program takes and returns all parts, laid end to end along the dimension named above; an argument that names none is the same for every part. Nothing has to cross between parts.
Inputs may be any that keep to these rules, and one draw needn't show every extreme that they name: `inverse`: A fixed matrix of order 2048. `section_three`: scenario s lies below section-2 node n = s // 128: its section-3 node is n * 16 + b with b from 0 to 15; every section-3 node holds exactly 8 scenarios.
All inputs are finite; a program needn't handle non-finite values.
Results may differ from a plain program's by a relative error of at most 0.0082.
Values may be sent and summed in bfloat16 or wider, within the bound.
A program may use at most 128 MiB of HBM per device.

v0:
```python
import jax
import jax.numpy as jnp
from jax import lax
from jax.sharding import PartitionSpec as P

BRANCH = 16


PENALTY = 1.0
CVAR_WEIGHT = 0.25
CVAR_LEVEL = 0.75


def partner(value, axis, stride):
    mask = 2**stride
    pairs = [(source, source ^ mask) for source in range(lax.axis_size(axis))]
    return lax.ppermute(value, axis, pairs)


def joined(own_part, peer_part, is_upper, along):
    return jnp.where(
        is_upper,
        jnp.concatenate((peer_part, own_part), along),
        jnp.concatenate((own_part, peer_part), along),
    )


def body(
    unit_costs,
    hour_duals,
    inverse,
    weights,
    section_three,
    prev_first,
    prev_second,
    prev_third,
    eta_mean,
    eta_duals,
):
    scenarios, hour_count, columns = unit_costs.shape
    section_len = hour_count // 3
    shares = BRANCH // 4
    my_index = lax.axis_index("node")
    quarter = my_index % 4
    second_table = prev_second
    third_table = prev_third
    for bit_num in range(2):
        is_upper = my_index // 2**bit_num % 2 == 1
        received = partner((second_table, third_table), "node", bit_num)
        second_table = joined(second_table, received[0], is_upper, 2)
        third_table = joined(third_table, received[1], is_upper, 0)
    choose = (section_three % BRANCH)[:, None] == jnp.arange(BRANCH, dtype=jnp.int32)[None, :]
    picker = choose.astype(jnp.bfloat16)
    third_anchor = jnp.dot(
        picker,
        third_table.reshape(BRANCH, section_len * columns),
        preferred_element_type=jnp.float32,
    )
    anchor = jnp.concatenate(
        (
            jnp.broadcast_to(
                prev_first.astype(jnp.float32)[None], (scenarios, section_len, columns)
            ),
            jnp.broadcast_to(
                second_table[0].astype(jnp.float32)[None], (scenarios, section_len, columns)
            ),
            third_anchor.reshape(scenarios, section_len, columns),
        ),
        axis=1,
    )
    target = (
        PENALTY * anchor - unit_costs.astype(jnp.float32) - hour_duals.astype(jnp.float32)
    ).astype(jnp.bfloat16)
    mass_vec = weights.astype(jnp.float32)
    mass_local = jnp.sum(mass_vec)
    flat = target.reshape(-1, columns)
    solution = jnp.dot(flat, inverse, preferred_element_type=jnp.float32).reshape(
        scenarios, -1, columns
    )
    first_part = jnp.sum(mass_vec[:, None, None] * solution[:, :section_len], axis=0)
    scen_cost = jnp.sum(unit_costs.astype(jnp.float32) * solution, axis=(1, 2)) / (
        hour_count * columns
    )
    low_end = eta_mean[0] - (CVAR_WEIGHT + eta_duals) / PENALTY
    high_end = low_end + CVAR_WEIGHT / ((1.0 - CVAR_LEVEL) * PENALTY)
    eta_value = jnp.minimum(jnp.maximum(scen_cost, low_end), high_end)
    first_sum, eta_total, mass_sum = lax.psum(
        (first_part, jnp.sum(mass_vec * eta_value), mass_local), "node"
    )
    weighted = choose.astype(jnp.float32) * mass_vec[:, None]
    third_part = jnp.dot(
        weighted.T,
        solution[:, 2 * section_len :].reshape(scenarios, section_len * columns),
        precision=lax.Precision.HIGHEST,
        preferred_element_type=jnp.float32,
    )
    third_mass = jnp.sum(weighted, axis=0)
    second_part = jnp.sum(
        mass_vec[:, None, None] * solution[:, section_len : 2 * section_len], axis=0
    )
    for bit_num in (1, 0):
        is_upper = my_index // 2**bit_num % 2 == 1
        half_cols = second_part.shape[1] // 2
        half_rows = third_part.shape[0] // 2
        keep_second = jnp.where(is_upper, second_part[:, half_cols:], second_part[:, :half_cols])
        send_second = jnp.where(is_upper, second_part[:, :half_cols], second_part[:, half_cols:])
        keep_third = jnp.where(is_upper, third_part[half_rows:], third_part[:half_rows])
        send_third = jnp.where(is_upper, third_part[:half_rows], third_part[half_rows:])
        received = partner((send_second, send_third, third_mass), "node", bit_num)
        second_part = keep_second + received[0]
        third_part = keep_third + received[1]
        third_mass = third_mass + received[2]
    own_mass = lax.dynamic_slice_in_dim(third_mass, quarter * shares, shares, 0)
    third_share = third_part / own_mass[:, None]
    second_share = second_part / jnp.sum(third_mass)
    second_whole = second_share
    third_whole = third_share
    for bit_num in range(2):
        is_upper = my_index // 2**bit_num % 2 == 1
        received = partner((second_whole, third_whole), "node", bit_num)
        second_whole = joined(second_whole, received[0], is_upper, 1)
        third_whole = joined(third_whole, received[1], is_upper, 0)
    first_avg = first_sum / mass_sum
    new_third = jnp.dot(
        choose.astype(jnp.float32),
        third_whole,
        precision=lax.Precision.HIGHEST,
        preferred_element_type=jnp.float32,
    ).reshape(scenarios, section_len, columns)
    new_anchor = jnp.concatenate(
        (
            jnp.broadcast_to(first_avg[None], (scenarios, section_len, columns)),
            jnp.broadcast_to(second_whole[None], (scenarios, section_len, columns)),
            new_third,
        ),
        axis=1,
    )
    duals_new = (hour_duals.astype(jnp.float32) + PENALTY * (solution - new_anchor)).astype(
        jnp.bfloat16
    )
    eta_level = eta_total / mass_sum
    eta_duals_new = eta_duals + PENALTY * (eta_value - eta_level)
    return (
        duals_new,
        first_avg,
        second_share[None],
        third_share.reshape(shares, section_len, columns),
        jnp.reshape(eta_level, (1,)),
        eta_duals_new,
    )


def solution(mesh):
    in_specs = (
        P(("groups", "node"), None, None),
        P(("groups", "node"), None, None),
        P(),
        P(("groups", "node")),
        P(("groups", "node")),
        P("groups", None),
        P(("groups", "node"), None, None),
        P(("groups", "node"), None, None),
        P("groups"),
        P(("groups", "node")),
    )
    out_specs = (
        P(("groups", "node"), None, None),
        P("groups", None),
        P(("groups", "node"), None, None),
        P(("groups", "node"), None, None),
        P("groups"),
        P(("groups", "node")),
    )
    return jax.shard_map(body, mesh=mesh, in_specs=in_specs, out_specs=out_specs, check_vma=False)
```

profile of v0, /device:TPU:0, one launch (start us, length us, event | category | flops | bytes accessed | tf_op | source)
XLA Modules:
  0.0 152.6 jit_solution(12685654493900703658)
XLA Ops:
  7.2 0.0 all-reduce.3.cloned.1.call-start
  7.2 0.5 collective-permute-start
  7.7 0.7 and_select_fusion
  8.4 0.7 convert_element_type.35
  9.1 0.1 select_reduce_fusion
  9.2 2.6 %collective-permute-start.6 = (f32[16]{0:T(128)S(1)}, f32[16]{0:T(128)S(1)}, u32[]{:S(2)}, u32[]{:S(2)}) collective-permute-start(f32[16]{0:T(128)S(1)} %select_reduce_fusion), channel_id=1, source_target_pairs={{0,2},{1,3},{2,0},{3,1},{4,6},{5,7},{6,4},{7,5},{8,10},{9,11},{10,... | collective-permute-start | bytes 200 | tf_op jit(solution)/shard_map/ppermute | solution.py:17
  11.8 0.2 collective-permute-start.2
  12.6 1.0 copy.21
  13.7 0.4 collective-permute-start.7
  14.0 0.8 maximum_select_fusion.9
  14.8 1.3 collective-permute-start.1
  16.1 0.8 maximum_select_fusion.10
  16.9 1.7 %collective-permute-done.1 = bf16[1,8,1024]{2,1,0:T(8,128)(2,1)S(1)} collective-permute-done((bf16[1,8,1024]{2,1,0:T(8,128)(2,1)S(1)}, bf16[1,8,1024]{2,1,0:T(8,128)(2,1)S(1)}, u32[]{:S(2)}, u32[]{:S(2)}) %collective-permute-start.1) | collective-permute-done | bytes 16416 | tf_op jit(solution)/shard_map/ppermute | solution.py:17
  18.6 0.1 copy.20
  18.7 1.0 maximum_select_fusion.4
  19.7 1.3 collective-permute-start.3
  21.1 0.2 maximum_select_fusion.5
  21.3 5.8 %collective-permute-done.3 = bf16[8,8,2048]{2,1,0:T(8,128)(2,1)S(1)} collective-permute-done((bf16[8,8,2048]{2,1,0:T(8,128)(2,1)S(1)}, bf16[8,8,2048]{2,1,0:T(8,128)(2,1)S(1)}, u32[]{:S(2)}, u32[]{:S(2)}) %collective-permute-start.3) | collective-permute-done | bytes 262176 | tf_op jit(solution)/shard_map/ppermute | solution.py:17
  27.1 0.1 copy.19
  27.2 0.1 maximum_select_fusion.2
  27.3 0.5 fusion.14
  27.8 1.2 copy.17
  29.0 0.2 broadcast_in_dim.11
  29.3 0.2 broadcast_in_dim.10
  29.5 0.2 copy-done.8
  29.7 1.4 copy-done.1
  31.1 9.9 %fusion.4 = (f32[32]{0:T(128)S(1)}, f32[32,24,2048]{2,1,0:T(8,128)S(1)}) fusion(bf16[32,24,2048]{2,1,0:T(8,128)(2,1)S(1)} %copy-done.8, bf16[2048,2048]{1,0:T(8,128)(2,1)} %param.12, bf16[32,24,2048]{2,1,0:T(8,128)(2,1)S(1)} %copy-done.1, f32[32,8,2048]{2,1,0:T(8,128)S(1)} %copy.17, f32[32,8,2048]{2,1,0:T(8,128)S(1)} %broadcast_in_dim.11, ...), kind=kOutput, calls=%fused_computation.8 | convolution fusion | flops 6458179584 | bytes 27263104 | tf_op jit(solution)/shard_map/dot_general | solution.py:77
  41.0 1.7 %fusion.7 = (f32[8,2048]{1,0:T(8,128)}, f32[8,2048]{1,0:T(8,128)S(1)}, f32[32,8,2048]{2,1,0:T(8,128)S(1)}) fusion(f32[32,24,2048]{2,1,0:T(8,128)S(1)} %get-tuple-element.17, f32[32]{0:T(128)S(1)} %convert_element_type.35), kind=kLoop, calls=%fused_computation.13 | loop fusion | flops 2064384 | bytes 8519808 | tf_op jit(solution)/shard_map/reduce_sum | solution.py:80
  42.7 0.9 copy-done
  43.7 1.2 copy.22
  44.9 1.1 fusion.19
  46.0 1.6 %collective-permute-start.4 = (f32[8,1024]{1,0:T(8,128)S(1)}, f32[8,1024]{1,0:T(8,128)S(1)}, u32[]{:S(2)}, u32[]{:S(2)}) collective-permute-start(f32[8,1024]{1,0:T(8,128)S(1)} %slice_select_fusion.2), channel_id=1, source_target_pairs={{0,2},{1,3},{2,0},{3,1},{4,6},{5,7},{6,4},{7,5},{8,10},{9,11},{10,... | collective-permute-start | bytes 98312 | tf_op jit(solution)/shard_map/ppermute | solution.py:17
  47.7 0.1 slice_select_fusion
  47.7 0.5 collective-permute-start.10
  48.3 0.6 fusion.32
  48.9 0.1 dynamic_slice.3
  48.9 0.0 all-reduce.3.cloned.1.call-update
  49.0 1.4 collective-permute-done.4
  50.4 0.1 collective-permute-start.5
  50.5 9.7 %collective-permute-done.10 = f32[8,16384]{1,0:T(8,128)S(1)} collective-permute-done((f32[8,16384]{1,0:T(8,128)S(1)}, f32[8,16384]{1,0:T(8,128)S(1)}, u32[]{:S(2)}, u32[]{:S(2)}) %collective-permute-start.10) | collective-permute-done | bytes 524320 | tf_op jit(solution)/shard_map/ppermute | solution.py:17
  60.2 0.1 select_add_fusion
  60.3 0.1 slice_select_fusion.1
  60.4 0.1 collective-permute-start.11
  60.5 0.6 multiply_reduce_fusion
  61.1 33.9 %all-reduce = (f32[]{:T(128)}, f32[]{:T(128)}) all-reduce(f32[]{:T(128)} %get-tuple-element.9, f32[]{:T(128)} %get-tuple-element.8), channel_id=1, replica_groups=mesh['groups'=2,'node'=16] {'node'}, use_global_device_ids=true, to_apply=%region_3.4 | all-reduce | flops 2 | bytes 16 | tf_op jit(solution)/shard_map/psum | solution.py:87
  96.3 0.7 add_divide_fusion.1
  97.0 0.1 collective-permute-start.8
  97.1 0.1 add_divide_fusion
  97.2 0.6 collective-permute-start.12
  97.8 0.5 subtract_add_fusion
  98.3 0.1 collective-permute-start.9
  98.4 0.6 collective-permute-done.12
  98.9 0.2 maximum_select_fusion.3
  99.1 1.5 collective-permute-start.13
  100.7 34.3 %all-reduce.3.cloned.1.call-done = f32[8,2048]{1,0:T(8,128)} async-done(((f32[8,2048]{1,0:T(8,128)}), f32[8,2048]{1,0:T(8,128)}) %all-reduce.3.cloned.1.call-update) | async-done | bytes 65552 | tf_op jit(solution)/shard_map/psum | solution.py:87
  134.9 1.5 broadcast_divide_fusion
  136.5 0.9 copy.30
  137.3 1.0 fusion.8
  138.4 1.2 copy.23
  139.6 0.2 broadcast_in_dim.13
  139.9 0.2 broadcast_in_dim.12
  140.1 0.3 slice-done.1
  140.4 1.2 copy-done.2
  141.7 2.9 %fusion.3 = bf16[32,24,2048]{2,1,0:T(8,128)(2,1)} fusion(bf16[32,24,2048]{2,1,0:T(8,128)(2,1)S(1)} %copy-done.2, f32[32,24,2048]{2,1,0:T(8,128)S(1)} %bitcast.36, f32[32,8,2048]{2,1,0:T(8,128)S(1)} %bitcast.37, f32[32,8,2048]{2,1,0:T(8,128)S(1)} %broadcast_in_dim.13, f32[32,8,2048]{2,1,0:T(8,128)S(1)} %broadcast_in_dim.12), kind=kLoop, calls=%fused_computation.7 | loop fusion | flops 9437184 | bytes 18874368 | tf_op jit(solution)/shard_map/convert_element_type | solution.py:138
  (34 shorter events, 0.1 us)
Async XLA Ops:
  7.2 127.8 %all-reduce.3.cloned.1.call-start = ((), (), s32[]{:S(2)}) async-start(), calls=%async_computation | async-start | bytes 131072 | tf_op jit(solution)/shard_map/psum | solution.py:87
  7.2 6.8 %collective-permute-start = (bf16[1,8,512]{2,1,0:T(8,128)(2,1)}, bf16[1,8,512]{2,1,0:T(8,128)(2,1)S(1)}, u32[]{:S(2)}, u32[]{:S(2)}) collective-permute-start(bf16[1,8,512]{2,1,0:T(8,128)(2,1)} %param.16), channel_id=1, source_target_pairs={{0,1},{1,0},{2,3},{3,2},{4,5},{5,4},{6,7},{7,6},{8,9},{9,8},{10,11... | collective-permute-start | bytes 24584 | tf_op jit(solution)/shard_map/ppermute | solution.py:17
  9.2 4.5 %collective-permute-start.6 = (f32[16]{0:T(128)S(1)}, f32[16]{0:T(128)S(1)}, u32[]{:S(2)}, u32[]{:S(2)}) collective-permute-start(f32[16]{0:T(128)S(1)} %select_reduce_fusion), channel_id=1, source_target_pairs={{0,2},{1,3},{2,0},{3,1},{4,6},{5,7},{6,4},{7,5},{8,10},{9,11},{10,... | collective-permute-start | bytes 200 | tf_op jit(solution)/shard_map/ppermute | solution.py:17
  11.8 6.8 %collective-permute-start.2 = (bf16[4,8,2048]{2,1,0:T(8,128)(2,1)}, bf16[4,8,2048]{2,1,0:T(8,128)(2,1)S(1)}, u32[]{:S(2)}, u32[]{:S(2)}) collective-permute-start(bf16[4,8,2048]{2,1,0:T(8,128)(2,1)} %param.17), channel_id=1, source_target_pairs={{0,1},{1,0},{2,3},{3,2},{4,5},{5,4},{6,7},{7,6},{8,9},{9,8},{10,11... | collective-permute-start | bytes 393224 | tf_op jit(solution)/shard_map/ppermute | solution.py:17
  13.7 34.6 %collective-permute-start.7 = (f32[16]{0:T(128)S(1)}, f32[16]{0:T(128)S(1)}, u32[]{:S(2)}, u32[]{:S(2)}) collective-permute-start(f32[16]{0:T(128)S(1)} %add.69), channel_id=1, source_target_pairs={{0,1},{1,0},{2,3},{3,2},{4,5},{5,4},{6,7},{7,6},{8,9},{9,8},{10,11... | collective-permute-start | bytes 200 | tf_op jit(solution)/shard_map/ppermute | solution.py:17
  14.8 3.7 %collective-permute-start.1 = (bf16[1,8,1024]{2,1,0:T(8,128)(2,1)S(1)}, bf16[1,8,1024]{2,1,0:T(8,128)(2,1)S(1)}, u32[]{:S(2)}, u32[]{:S(2)}) collective-permute-start(bf16[1,8,1024]{2,1,0:T(8,128)(2,1)S(1)} %maximum_select_fusion.9), channel_id=1, source_target_pairs={{0,2},{1,3},{2,0},{3,1},{4,6},{5,7},{6,4},{7,5},{8,10},{9,11},{10,... | collective-permute-start | bytes 49160 | tf_op jit(solution)/shard_map/ppermute | solution.py:17
  19.7 7.3 %collective-permute-start.3 = (bf16[8,8,2048]{2,1,0:T(8,128)(2,1)S(1)}, bf16[8,8,2048]{2,1,0:T(8,128)(2,1)S(1)}, u32[]{:S(2)}, u32[]{:S(2)}) collective-permute-start(bf16[8,8,2048]{2,1,0:T(8,128)(2,1)S(1)} %maximum_select_fusion.4), channel_id=1, source_target_pairs={{0,2},{1,3},{2,0},{3,1},{4,6},{5,7},{6,4},{7,5},{8,10},{9,11},{10,... | collective-permute-start | bytes 786440 | tf_op jit(solution)/shard_map/ppermute | solution.py:17
  27.8 1.5 copy-start.5
  27.8 1.9 %copy-start.8 = (bf16[32,24,2048]{2,1,0:T(8,128)(2,1)S(1)}, bf16[32,24,2048]{2,1,0:T(8,128)(2,1)}, u32[]{:S(2)}) copy-start(bf16[32,24,2048]{2,1,0:T(8,128)(2,1)} %param.10) | copy-start | bytes 9437188
  29.0 2.1 %copy-start.1 = (bf16[32,24,2048]{2,1,0:T(8,128)(2,1)S(1)}, bf16[32,24,2048]{2,1,0:T(8,128)(2,1)}, u32[]{:S(2)}) copy-start(bf16[32,24,2048]{2,1,0:T(8,128)(2,1)} %param.11) | copy-start | bytes 9437188
  41.0 2.7 %copy-start = (f32[32,24,2048]{2,1,0:T(8,128)}, f32[32,24,2048]{2,1,0:T(8,128)S(1)}, u32[]{:S(2)}) copy-start(f32[32,24,2048]{2,1,0:T(8,128)S(1)} %get-tuple-element.17) | copy-start | bytes 18874372
  46.0 14.4 %copy-start.6 = (f32[32]{0:T(128)S(1)}, f32[32]{0:T(128)}, u32[]{:S(2)}) copy-start(f32[32]{0:T(128)} %param.19) | copy-start | bytes 388
  46.0 14.4 %copy-start.7 = (s32[32]{0:T(128)S(1)}, s32[32]{0:T(128)}, u32[]{:S(2)}) copy-start(s32[32]{0:T(128)} %param.13) | copy-start | bytes 388
  46.0 4.3 %collective-permute-start.4 = (f32[8,1024]{1,0:T(8,128)S(1)}, f32[8,1024]{1,0:T(8,128)S(1)}, u32[]{:S(2)}, u32[]{:S(2)}) collective-permute-start(f32[8,1024]{1,0:T(8,128)S(1)} %slice_select_fusion.2), channel_id=1, source_target_pairs={{0,2},{1,3},{2,0},{3,1},{4,6},{5,7},{6,4},{7,5},{8,10},{9,11},{10,... | collective-permute-start | bytes 98312 | tf_op jit(solution)/shard_map/ppermute | solution.py:17
  47.7 12.5 %collective-permute-start.10 = (f32[8,16384]{1,0:T(8,128)S(1)}, f32[8,16384]{1,0:T(8,128)S(1)}, u32[]{:S(2)}, u32[]{:S(2)}) collective-permute-start(f32[8,16384]{1,0:T(8,128)S(1)} %slice_select_fusion), channel_id=1, source_target_pairs={{0,2},{1,3},{2,0},{3,1},{4,6},{5,7},{6,4},{7,5},{8,10},{9,11},{10,... | collective-permute-start | bytes 1572872 | tf_op jit(solution)/shard_map/ppermute | solution.py:17
  50.4 45.9 %collective-permute-start.5 = (f32[8,512]{1,0:T(8,128)S(1)}, f32[8,512]{1,0:T(8,128)S(1)}, u32[]{:S(2)}, u32[]{:S(2)}) collective-permute-start(f32[8,512]{1,0:T(8,128)S(1)} %slice_select_fusion.3), channel_id=1, source_target_pairs={{0,1},{1,0},{2,3},{3,2},{4,5},{5,4},{6,7},{7,6},{8,9},{9,8},{10,11... | collective-permute-start | bytes 49160 | tf_op jit(solution)/shard_map/ppermute | solution.py:17
  60.4 36.7 %collective-permute-start.11 = (f32[4,16384]{1,0:T(4,128)S(1)}, f32[4,16384]{1,0:T(4,128)S(1)}, u32[]{:S(2)}, u32[]{:S(2)}) collective-permute-start(f32[4,16384]{1,0:T(4,128)S(1)} %slice_select_fusion.1), channel_id=1, source_target_pairs={{0,1},{1,0},{2,3},{3,2},{4,5},{5,4},{6,7},{7,6},{8,9},{9,8},{10,11... | collective-permute-start | bytes 786440 | tf_op jit(solution)/shard_map/ppermute | solution.py:17
  97.0 42.6 %copy-start.4 = (f32[8,512]{1,0:T(8,128)}, f32[8,512]{1,0:T(8,128)S(1)}, u32[]{:S(2)}) copy-start(f32[8,512]{1,0:T(8,128)S(1)} %add_divide_fusion.1) | copy-start | bytes 49156
  97.0 1.3 collective-permute-start.8
  97.2 1.7 %collective-permute-start.12 = (f32[4,16384]{1,0:T(4,128)S(1)}, f32[4,16384]{1,0:T(4,128)S(1)}, u32[]{:S(2)}, u32[]{:S(2)}) collective-permute-start(f32[4,16384]{1,0:T(4,128)S(1)} %add_divide_fusion), channel_id=1, source_target_pairs={{0,1},{1,0},{2,3},{3,2},{4,5},{5,4},{6,7},{7,6},{8,9},{9,8},{10,11... | collective-permute-start | bytes 786440 | tf_op jit(solution)/shard_map/ppermute | solution.py:17
  98.3 38.1 %collective-permute-start.9 = (f32[8,1024]{1,0:T(8,128)S(1)}, f32[8,1024]{1,0:T(8,128)S(1)}, u32[]{:S(2)}, u32[]{:S(2)}) collective-permute-start(f32[8,1024]{1,0:T(8,128)S(1)} %maximum_select_fusion.8), channel_id=1, source_target_pairs={{0,2},{1,3},{2,0},{3,1},{4,6},{5,7},{6,4},{7,5},{8,10},{9,11},{10,... | collective-permute-start | bytes 98312 | tf_op jit(solution)/shard_map/ppermute | solution.py:17
  99.1 38.2 %collective-permute-start.13 = (f32[8,16384]{1,0:T(8,128)S(1)}, f32[8,16384]{1,0:T(8,128)S(1)}, u32[]{:S(2)}, u32[]{:S(2)}) collective-permute-start(f32[8,16384]{1,0:T(8,128)S(1)} %maximum_select_fusion.3), channel_id=1, source_target_pairs={{0,2},{1,3},{2,0},{3,1},{4,6},{5,7},{6,4},{7,5},{8,10},{9,11},{10,... | collective-permute-start | bytes 1572872 | tf_op jit(solution)/shard_map/ppermute | solution.py:17
  136.4 3.5 %copy-start.3 = (f32[8,2048]{1,0:T(8,128)}, f32[8,2048]{1,0:T(8,128)S(1)}, u32[]{:S(2)}) copy-start(f32[8,2048]{1,0:T(8,128)S(1)} %broadcast_divide_fusion) | copy-start | bytes 196612
  137.3 2.8 %slice-start = ((s8[6291456]{0:T(1024)(128)(4,1)}), s8[4194304]{0:T(1024)(128)(4,1)S(1)}, s32[]{:S(2)}) async-start(s8[6291456]{0:T(1024)(128)(4,1)} %bitcast.35), calls=%async_computation.1 | async-start | bytes 8388608
  138.4 2.0 %slice-start.1 = ((s8[6291456]{0:T(1024)(128)(4,1)}), s8[2097152]{0:T(1024)(128)(4,1)S(1)}, s32[]{:S(2)}) async-start(s8[6291456]{0:T(1024)(128)(4,1)} %bitcast.35), calls=%async_computation.2 | async-start | bytes 4194304
  139.6 2.0 %copy-start.2 = (bf16[32,24,2048]{2,1,0:T(8,128)(2,1)S(1)}, bf16[32,24,2048]{2,1,0:T(8,128)(2,1)}, u32[]{:S(2)}) copy-start(bf16[32,24,2048]{2,1,0:T(8,128)(2,1)} %param.11) | copy-start | bytes 9437188
Sparse Core Ops, SparseCore 0:
  49.1 85.7 all-reduce.2
where the time goes:
time: 154 us; the launch traced here: 153 us
  waiting for transfers between devices  53.4 us (35%)
  blocking collectives  33.9 us (22%)
  between operations  17.5 us (11%)
  other arithmetic  13.4 us (9%)
  matrix products  12.5 us (8%)
  starting transfers between devices  10.9 us (7%)
  local copies, waits for them, and re-layouts  10.9 us (7%)
    psum x1, waiting for transfers between devices, body(): lax.psum((first_part, jnp.sum(mass_vec * eta_value), mass_local), 'node')  34.3 us
    psum x1, blocking collectives, body(): lax.psum((first_part, jnp.sum(mass_vec * eta_value), mass_local), 'node')  33.9 us
    ppermute x14, waiting for transfers between devices, partner(): return lax.ppermute(value, axis, pairs)  19.2 us
    ppermute x14, starting transfers between devices, partner(): return lax.ppermute(value, axis, pairs)  10.8 us
    dot_general x1, matrix products, body(): jnp.dot(flat, inverse, preferred_element_type=jnp.float32)  9.87 us
    unnamed x28, local copies, waits for them, and re-layouts  8.66 us
    select_n x8, other arithmetic, joined(): jnp.where(is_upper, jnp.concatenate((peer_part, own_part), along), jnp.co...  3.12 us
  transfers between devices with their start and end apart: 15, of which 6 were waited for; matrix products, arithmetic and copies ran while one was open for 18% of the time, Pallas kernels for 0%

commit v1 on v0

v1 whole, which is shorter than its diff:
```python
import functools

import jax
import jax.numpy as jnp
from jax import lax
from jax.experimental import pallas as pl
from jax.experimental.pallas import tpu as pltpu
from jax.sharding import PartitionSpec as P

BRANCH = 16
PENALTY = 1.0
CVAR_WEIGHT = 0.25
CVAR_LEVEL = 0.75
CHUNKS = 4
MESH = pl.DeviceIdType.MESH
F32 = jnp.float32
BF16 = jnp.bfloat16


def kernel(
    n,
    c_hbm,
    d_hbm,
    inv_hbm,
    w_ref,
    b_ref,
    b_smem,
    pf_ref,
    ps_ref,
    pt_hbm,
    em_ref,
    ed_ref,
    duals_ref,
    first_ref,
    second_ref,
    third_ref,
    level_ref,
    ednew_ref,
    c_ref,
    d_ref,
    inv_ref,
    t_ref,
    x_ref,
    s_ref,
    w_mat,
    tab_ref,
    avg_ref,
    tl_ref,
    pt_tab,
    sec_tab,
    meta_ref,
    eta_ref,
    x1_send,
    x1_recv,
    x2_send,
    x2_recv,
    fs_send,
    fs_recv,
    z_ref,
    cost_ref,
    load_sem,
    meta_ssem,
    meta_rsem,
    eta_ssem,
    eta_rsem,
    pt_ssem,
    pt_rsem,
    sec_ssem,
    sec_rsem,
    x1_ssem,
    x1_rsem,
    x2_ssem,
    x2_rsem,
    x3_ssem,
    x3_rsem,
    fs_ssem,
    fs_rsem,
    z_ssem,
    z_rsem,
    ag_ssem,
    ag_rsem,
):
    rows, cols = c_ref.shape
    scen = b_smem.shape[0]
    hours = rows // scen
    hs = hours // 3
    groups2 = n // 4
    width = cols // CHUNKS
    quart = cols // 4
    tile = min(256, width)
    half = BRANCH * hs // 2
    me = lax.axis_index("node")
    quarter = lax.rem(me, 4)
    core = lax.rem(me, 2)
    base = me - quarter
    team = lax.div(me, 4)
    core_peer = me + 1 - 2 * core
    far_peer = me + 2 - 4 * lax.rem(lax.div(me, 2), 2)
    far_q = lax.rem(quarter + 2, 4)
    core_q = quarter + 1 - 2 * core
    diag_q = lax.rem(core_q + 2, 4)

    def remote(src, dst, ssem, rsem, device):
        return pltpu.make_async_remote_copy(
            src_ref=src,
            dst_ref=dst,
            send_sem=ssem,
            recv_sem=rsem,
            device_id={"node": device},
            device_id_type=MESH,
        )

    def chunk(k):
        return pl.ds(k * width, width)

    def load(k, which):
        src, dst = ((c_hbm, c_ref), (d_hbm, d_ref), (inv_hbm, inv_ref))[which]
        return pltpu.make_async_copy(
            src.at[:, chunk(k)], dst.at[:, chunk(k)], load_sem.at[which, k]
        )

    for k in range(CHUNKS):
        load(k, 0).start()
        load(k, 1).start()
    for k in range(CHUNKS):
        load(k, 2).start()
    own_third = pltpu.make_async_copy(pt_hbm, pt_tab.at[quarter], load_sem.at[3, 0])
    own_third.start()

    barrier = pltpu.get_barrier_semaphore()

    @pl.loop(1, n)
    def _(r):
        pl.semaphore_signal(
            barrier, inc=1, device_id={"node": lax.rem(me + r, n)}, device_id_type=MESH
        )

    weight_row = w_ref[...].astype(F32)
    branch_row = lax.rem(b_ref[...], BRANCH).astype(F32)
    meta_ref[me] = jnp.zeros(meta_ref.shape[1:], F32)
    meta_ref[me, 0:1, 0:scen] = weight_row
    meta_ref[me, 1:2, 0:scen] = branch_row
    sec_tab[quarter] = ps_ref[...].astype(F32)
    pl.semaphore_wait(barrier, n - 1)

    third_far = remote(
        pt_hbm, pt_tab.at[quarter], pt_ssem.at[0], pt_rsem.at[0], far_peer
    )
    third_core = remote(
        pt_hbm, pt_tab.at[quarter], pt_ssem.at[1], pt_rsem.at[1], core_peer
    )
    third_pass = remote(
        pt_tab.at[far_q], pt_tab.at[far_q], pt_ssem.at[2], pt_rsem.at[2], core_peer
    )
    third_far.start()
    third_core.start()

    def meta_copy(r):
        return remote(
            meta_ref.at[me],
            meta_ref.at[me],
            meta_ssem.at[r],
            meta_rsem.at[r],
            lax.rem(me + r, n),
        )

    @pl.loop(1, n)
    def _(r):
        meta_copy(r).start()

    def sec_copy(r):
        return remote(
            sec_tab.at[quarter],
            sec_tab.at[quarter],
            sec_ssem.at[r],
            sec_rsem.at[r],
            base + lax.rem(quarter + r, 4),
        )

    for r in range(1, 4):
        sec_copy(r).start()

    lane = lax.broadcasted_iota(jnp.int32, (scen, rows), 1)
    low = lax.broadcasted_iota(jnp.int32, (scen, rows), 0) * hours
    spread = jnp.where((lane >= low) & (lane < low + hours), 1.0, 0.0).astype(BF16)
    small = jnp.concatenate(
        (
            weight_row,
            branch_row,
            lax.broadcasted_iota(jnp.int32, (1, scen), 1).astype(F32),
            jnp.zeros((5, scen), F32),
        ),
        axis=0,
    ).astype(BF16)
    wide = jnp.dot(small, spread, preferred_element_type=F32)
    hour = lax.broadcasted_iota(jnp.int32, (1, rows), 1).astype(F32) - hours * wide[2:3]
    place = hour + jnp.where(hour >= 2.0 * hs, hs * wide[1:2], 0.0)
    line = lax.broadcasted_iota(jnp.int32, w_mat.shape, 0).astype(F32)
    w_mat[...] = jnp.where(place == line, wide[0:1], 0.0).astype(BF16)

    def x1_copy(k):
        return remote(
            x1_send.at[k], x1_recv.at[k], x1_ssem.at[k], x1_rsem.at[k], core_peer
        )

    def x2_copy(k):
        return remote(
            x2_send.at[k], x2_recv.at[k], x2_ssem.at[k], x2_rsem.at[k], far_peer
        )

    own_rows = pl.ds(pl.multiple_of(2 * hs + half * core, 16), half)
    peer_rows = pl.ds(pl.multiple_of(2 * hs + half * (1 - core), 16), half)
    for k in range(CHUNKS):
        load(k, 0).wait()
        load(k, 1).wait()
        s_ref[:, chunk(k)] = jnp.dot(
            w_mat[...], c_ref[:, chunk(k)], preferred_element_type=F32
        ) + jnp.dot(w_mat[...], d_ref[:, chunk(k)], preferred_element_type=F32)
        x1_send[k] = s_ref[peer_rows, chunk(k)].astype(BF16)
        x1_copy(k).start()
    for j in range(4):
        fs_send[j] = s_ref[0 : 2 * hs, j * quart : (j + 1) * quart].astype(BF16)

    def fs_copy(r):
        to = lax.rem(quarter + r, 4)
        return remote(
            fs_send.at[to], fs_recv.at[r], fs_ssem.at[r], fs_rsem.at[r], base + to
        )

    for r in range(1, 4):
        fs_copy(r).start()

    third_far.wait_recv()
    third_pass.start()

    for k in range(CHUNKS):
        x1_copy(k).wait_recv()
        s_ref[own_rows, chunk(k)] = s_ref[own_rows, chunk(k)] + x1_recv[k].astype(F32)
        x2_send[k] = s_ref[own_rows, chunk(k)].astype(BF16)
        x2_copy(k).start()

    my_cols = pl.ds(pl.multiple_of(quarter * quart, 128), quart)
    pair = s_ref[0 : 2 * hs, my_cols]
    for r in range(1, 4):
        fs_copy(r).wait_recv()
        pair = pair + fs_recv[r].astype(F32)
    z_ref[team] = pair[0:hs]

    def z_copy(r):
        return remote(
            z_ref.at[team],
            z_ref.at[team],
            z_ssem.at[r],
            z_rsem.at[r],
            lax.rem(team + r, groups2) * 4 + quarter,
        )

    for r in range(1, groups2):
        z_copy(r).start()

    tab_ref[0] = pf_ref[...].astype(F32)
    for r in range(1, 4):
        sec_copy(r).wait_recv()
    for j in range(4):
        tab_ref[1, :, j * quart : (j + 1) * quart] = sec_tab[j]
    own_third.wait()
    third_core.wait_recv()
    third_pass.wait_recv()
    for j in range(4):
        tab_ref[2 + 4 * j : 6 + 4 * j] = pt_tab[j].astype(F32).reshape(4, hs, cols)

    @pl.loop(0, scen // 2)
    def _(i):
        window = pl.ds(pl.multiple_of(i * 2 * hours, 16), 2 * hours)
        b0 = lax.rem(b_smem[2 * i], BRANCH)
        b1 = lax.rem(b_smem[2 * i + 1], BRANCH)
        for k in range(CHUNKS):
            first = tab_ref[0, :, chunk(k)]
            second = tab_ref[1, :, chunk(k)]
            anchor = jnp.concatenate(
                (
                    first,
                    second,
                    tab_ref[2 + b0, :, chunk(k)],
                    first,
                    second,
                    tab_ref[2 + b1, :, chunk(k)],
                ),
                axis=0,
            )
            t_ref[window, chunk(k)] = (
                PENALTY * anchor
                - c_ref[window, chunk(k)].astype(F32)
                - d_ref[window, chunk(k)].astype(F32)
            ).astype(BF16)

    cost_ref[...] = jnp.zeros_like(cost_ref)

    def product(k):
        load(k, 2).wait()

        @pl.loop(0, width // tile)
        def _(j):
            part = pl.ds(pl.multiple_of(k * width + j * tile, 128), tile)
            x = jnp.dot(t_ref[...], inv_ref[:, part], preferred_element_type=F32)
            x_ref[:, part] = x
            y = x * c_ref[:, part].astype(F32)
            cost = cost_ref[...]
            for e in range(tile // 128):
                cost = cost + y[:, e * 128 : (e + 1) * 128]
            cost_ref[...] = cost

    product(0)

    @pl.loop(1, n)
    def _(r):
        meta_copy(r).wait_recv()

    mass_all = jnp.sum(meta_ref[:, 0, :])
    mass_two = jnp.zeros((), F32)
    node_line = lax.broadcasted_iota(jnp.int32, (BRANCH * hs, 128), 0).astype(F32)
    mass_lanes = jnp.zeros((BRANCH * hs, 128), F32)
    for j in range(4):
        w_j = meta_ref[base + j, 0:1, :]
        b_j = meta_ref[base + j, 1:2, :] * hs
        mass_two = mass_two + jnp.sum(w_j)
        mass_lanes = mass_lanes + jnp.where(
            (node_line >= b_j) & (node_line < b_j + hs), w_j, 0.0
        )
    s_ref[2 * hs :, cols : cols + 128] = jnp.broadcast_to(
        jnp.sum(mass_lanes, axis=1, keepdims=True), mass_lanes.shape
    )
    for r in range(1, groups2):
        z_copy(r).wait_recv()
    total = z_ref[0]
    for g in range(1, groups2):
        total = total + z_ref[g]
    tl_ref[0 : 2 * hs, my_cols] = jnp.concatenate(
        (
            PENALTY * tab_ref[0, :, my_cols] - total / mass_all,
            PENALTY * tab_ref[1, :, my_cols] - pair[hs:] / mass_two,
        ),
        axis=0,
    ).astype(BF16)

    def ag_copy(r):
        return remote(
            tl_ref.at[0 : 2 * hs, my_cols],
            tl_ref.at[0 : 2 * hs, my_cols],
            ag_ssem.at[r],
            ag_rsem.at[r],
            base + lax.rem(quarter + r, 4),
        )

    for r in range(1, 4):
        ag_copy(r).start()

    for k in range(1, CHUNKS):
        product(k)

    by_scen = jnp.sum(cost_ref[...].reshape(scen, hours, 128), axis=1)
    cost_row = lax.dot_general(
        jnp.ones((8, 128), F32),
        by_scen,
        (((1,), (1,)), ((), ())),
        precision=lax.Precision.HIGHEST,
        preferred_element_type=F32,
    )[0:1] / (hours * cols)
    low_end = em_ref[0] - (CVAR_WEIGHT + ed_ref[...]) / PENALTY
    high_end = low_end + CVAR_WEIGHT / ((1.0 - CVAR_LEVEL) * PENALTY)
    eta = jnp.minimum(jnp.maximum(cost_row, low_end), high_end)
    eta_ref[me] = jnp.broadcast_to(
        jnp.sum(weight_row * eta, axis=1, keepdims=True), eta_ref.shape[1:]
    )

    def eta_copy(r):
        return remote(
            eta_ref.at[me],
            eta_ref.at[me],
            eta_ssem.at[r],
            eta_rsem.at[r],
            lax.rem(me + r, n),
        )

    @pl.loop(1, n)
    def _(r):
        eta_copy(r).start()

    def x3_copy(k):
        return remote(
            tl_ref.at[own_rows, chunk(k)],
            tl_ref.at[own_rows, chunk(k)],
            x3_ssem.at[k],
            x3_rsem.at[k],
            core_peer,
        )

    own_mass = s_ref[own_rows, cols : cols + 1]
    own_nodes = pl.ds(2 + (BRANCH // 2) * core, BRANCH // 2)
    for k in range(CHUNKS):
        x2_copy(k).wait_recv()
        mean = (s_ref[own_rows, chunk(k)] + x2_recv[k].astype(F32)) / own_mass
        anchor = tab_ref[own_nodes, :, chunk(k)].reshape(half, width)
        tl_ref[own_rows, chunk(k)] = (PENALTY * anchor - mean).astype(BF16)
        x3_copy(k).start()
    for r in range(1, 4):
        ag_copy(r).wait_recv()
    for k in range(CHUNKS):
        x3_copy(k).wait_recv()

    @pl.loop(0, cols // tile)
    def _(j):
        part = pl.ds(pl.multiple_of(j * tile, 128), tile)
        avg_ref[:, :, part] = jnp.dot(
            tl_ref[...], inv_ref[:, part], preferred_element_type=F32
        ).reshape(avg_ref.shape[0], hs, tile)

    @pl.loop(0, scen // 2)
    def _(i):
        window = pl.ds(pl.multiple_of(i * 2 * hours, 16), 2 * hours)
        b0 = lax.rem(b_smem[2 * i], BRANCH)
        b1 = lax.rem(b_smem[2 * i + 1], BRANCH)
        for k in range(CHUNKS):
            first = avg_ref[0, :, chunk(k)]
            second = avg_ref[1, :, chunk(k)]
            mean = jnp.concatenate(
                (
                    first,
                    second,
                    avg_ref[2 + b0, :, chunk(k)],
                    first,
                    second,
                    avg_ref[2 + b1, :, chunk(k)],
                ),
                axis=0,
            )
            duals_ref[window, chunk(k)] = (
                d_ref[window, chunk(k)].astype(F32)
                + PENALTY * (x_ref[window, chunk(k)] - mean)
            ).astype(BF16)

    first_ref[...] = avg_ref[0]
    second_ref[...] = avg_ref[1, :, my_cols]
    third_ref[...] = avg_ref[pl.ds(2 + 4 * quarter, 4)].reshape(4 * hs, cols)

    @pl.loop(1, n)
    def _(r):
        eta_copy(r).wait_recv()

    level = eta_ref[0]
    for g in range(1, n):
        level = level + eta_ref[g]
    level = level / mass_all
    level_ref[...] = level[0:1, 0:1]
    ednew_ref[...] = ed_ref[...] + PENALTY * (eta - level[0:1, 0:scen])

    @pl.loop(1, n)
    def _(r):
        meta_copy(r).wait_send()
        eta_copy(r).wait_send()

    for copy in (third_far, third_core, third_pass):
        copy.wait_send()
    for r in range(1, 4):
        sec_copy(r).wait_send()
        fs_copy(r).wait_send()
        ag_copy(r).wait_send()
    for r in range(1, groups2):
        z_copy(r).wait_send()
    for k in range(CHUNKS):
        x1_copy(k).wait_send()
        x2_copy(k).wait_send()
        x3_copy(k).wait_send()


def body(
    n,
    unit_costs,
    hour_duals,
    inverse,
    weights,
    section_three,
    prev_first,
    prev_second,
    prev_third,
    eta_mean,
    eta_duals,
):
    scen, hours, cols = unit_costs.shape
    hs = hours // 3
    rows = scen * hours
    lines = 2 * hs + BRANCH * hs
    width, quart = cols // CHUNKS, cols // 4
    half = BRANCH * hs // 2
    vmem = pl.BlockSpec(memory_space=pltpu.VMEM)
    smem = pl.BlockSpec(memory_space=pltpu.SMEM)
    anywhere = pl.BlockSpec(memory_space=pl.ANY)
    dma = pltpu.SemaphoreType.DMA
    outs = pl.pallas_call(
        functools.partial(kernel, n),
        out_shape=(
            jax.ShapeDtypeStruct((rows, cols), BF16),
            jax.ShapeDtypeStruct((hs, cols), F32),
            jax.ShapeDtypeStruct((hs, quart), F32),
            jax.ShapeDtypeStruct((4 * hs, cols), F32),
            jax.ShapeDtypeStruct((1, 1), F32),
            jax.ShapeDtypeStruct((1, scen), F32),
        ),
        in_specs=[
            anywhere,
            anywhere,
            anywhere,
            vmem,
            vmem,
            smem,
            vmem,
            vmem,
            anywhere,
            smem,
            vmem,
        ],
        out_specs=(vmem,) * 6,
        scratch_shapes=[
            pltpu.VMEM((rows, cols), BF16),
            pltpu.VMEM((rows, cols), BF16),
            pltpu.VMEM((cols, cols), BF16),
            pltpu.VMEM((rows, cols), BF16),
            pltpu.VMEM((rows, cols), F32),
            pltpu.VMEM((lines, cols + 128), F32),
            pltpu.VMEM((lines, rows), BF16),
            pltpu.VMEM((lines // hs, hs, cols), F32),
            pltpu.VMEM((lines // hs, hs, cols), F32),
            pltpu.VMEM((lines, cols), BF16),
            pltpu.VMEM((4, 4 * hs, cols), BF16),
            pltpu.VMEM((4, hs, quart), F32),
            pltpu.VMEM((n, 8, 128), F32),
            pltpu.VMEM((n, 8, 128), F32),
            pltpu.VMEM((CHUNKS, half, width), BF16),
            pltpu.VMEM((CHUNKS, half, width), BF16),
            pltpu.VMEM((CHUNKS, half, width), BF16),
            pltpu.VMEM((CHUNKS, half, width), BF16),
            pltpu.VMEM((4, 2 * hs, quart), BF16),
            pltpu.VMEM((4, 2 * hs, quart), BF16),
            pltpu.VMEM((n // 4, hs, quart), F32),
            pltpu.VMEM((rows, 128), F32),
            dma((4, CHUNKS)),
            dma((n,)),
            dma((n,)),
            dma((n,)),
            dma((n,)),
            dma((3,)),
            dma((3,)),
            dma((4,)),
            dma((4,)),
            dma((CHUNKS,)),
            dma((CHUNKS,)),
            dma((CHUNKS,)),
            dma((CHUNKS,)),
            dma((CHUNKS,)),
            dma((CHUNKS,)),
            dma((4,)),
            dma((4,)),
            dma((n // 4,)),
            dma((n // 4,)),
            dma((4,)),
            dma((4,)),
        ],
        compiler_params=pltpu.CompilerParams(
            collective_id=0, has_side_effects=True, vmem_limit_bytes=52 * 2**20
        ),
    )(
        unit_costs.reshape(rows, cols),
        hour_duals.reshape(rows, cols),
        inverse,
        weights.reshape(1, scen),
        section_three.reshape(1, scen),
        section_three,
        prev_first,
        prev_second.reshape(hs, quart),
        prev_third.reshape(4 * hs, cols),
        eta_mean,
        eta_duals.reshape(1, scen),
    )
    duals_new, first_avg, second_avg, third_avg, level, eta_new = outs
    return (
        duals_new.reshape(scen, hours, cols),
        first_avg,
        second_avg.reshape(1, hs, quart),
        third_avg.reshape(4, hs, cols),
        level.reshape(1),
        eta_new.reshape(scen),
    )


def solution(mesh):
    both = ("groups", "node")
    cube = P(both, None, None)
    in_specs = (
        cube,
        cube,
        P(),
        P(both),
        P(both),
        P("groups", None),
        cube,
        cube,
        P("groups"),
        P(both),
    )
    out_specs = (cube, P("groups", None), cube, cube, P("groups"), P(both))
    return jax.shard_map(
        functools.partial(body, mesh.shape["node"]),
        mesh=mesh,
        in_specs=in_specs,
        out_specs=out_specs,
        check_vma=False,
    )
```

time: 154 us -> 45.2 us (0.29)
  waiting for transfers between devices: 53.4 us -> 0 us
  blocking collectives: 33.9 us -> 0 us
  Pallas kernels: 0 us -> 31.2 us
  between operations: 17.5 us -> 3 us
  other arithmetic: 13.4 us -> 0 us
  matrix products: 12.5 us -> 0 us
  starting transfers between devices: 10.9 us -> 0 us
    psum x1 -> x0, waiting for transfers between devices: 34.3 us -> none  [body(): lax.psum((first_part, jnp.sum(mass_vec * eta_value), mass_local), 'node')]
    psum x1 -> x0, blocking collectives: 33.9 us -> none  [body(): lax.psum((first_part, jnp.sum(mass_vec * eta_value), mass_local), 'node')]
    pallas_call x0 -> x1, Pallas kernels: none -> 31.2 us  [body(): pl.pallas_call(functools.partial(kernel, n), out_shape=(jax.ShapeDtypeStr...]
    ppermute x14 -> x0, waiting for transfers between devices: 19.2 us -> none  [partner(): return lax.ppermute(value, axis, pairs)]
    dot_general x4 -> x0, matrix products: 12.5 us -> none  [the longest x1 9.87 us: body(): jnp.dot(flat, inverse, preferred_element_type=jnp.float32)]
    ppermute x14 -> x0, starting transfers between devices: 10.8 us -> none  [partner(): return lax.ppermute(value, axis, pairs)]
    select_n x13 -> x0, other arithmetic: 3.92 us -> none  [the longest x8 3.12 us: joined(): jnp.where(is_upper, jnp.concatenate((peer_part, own_part), along), jnp.co...]
    convert_element_type x3 -> x0, other arithmetic: 3.58 us -> none  [the longest x1 2.91 us: body(): (hour_duals.astype(jnp.float32) + PENALTY * (solution - new_anchor)).asty...]
  transfers between devices with their start and end apart: 15 -> 0, of which waited for: 6 -> 0; matrix products, arithmetic and copies ran while one was open for 18% -> 0% of each run, Pallas kernels for 0% -> 0%
where the time goes in v1:
time: 45.2 us; the launch traced here: 44.9 us
  Pallas kernels  31.2 us (69%)
  local copies, waits for them, and re-layouts  10.7 us (24%)
  between operations  3 us (7%)
    pallas_call x1, Pallas kernels, body(): pl.pallas_call(functools.partial(kernel, n), out_shape=(jax.ShapeDtypeStr...  31.2 us
    unnamed x17, local copies, waits for them, and re-layouts  10.7 us

profile of v1, /device:TPU:0, one launch (start us, length us, event | category | flops | bytes accessed | tf_op | source)
XLA Modules:
  0.0 44.9 jit_solution(3662644624835620524)
XLA Ops:
  1.3 0.0 copy-start
  1.3 0.9 %copy-done = bf16[4,8,2048]{2,1,0:T(8,128)(2,1)S(1)} copy-done((bf16[4,8,2048]{2,1,0:T(8,128)(2,1)S(1)}, bf16[4,8,2048]{2,1,0:T(8,128)(2,1)}, u32[]{:S(2)}) %copy-start) | copy-done | bytes 131096
  2.2 0.0 copy-start.1
  2.2 0.8 %copy-done.1 = bf16[8,2048]{1,0:T(8,128)(2,1)S(1)} copy-done((bf16[8,2048]{1,0:T(8,128)(2,1)S(1)}, bf16[8,2048]{1,0:T(8,128)(2,1)}, u32[]{:S(2)}) %copy-start.1) | copy-done | bytes 32792
  2.9 0.0 copy-start.2
  2.9 0.7 %copy-done.2 = bf16[1,8,512]{2,1,0:T(8,128)(2,1)S(1)} copy-done((bf16[1,8,512]{2,1,0:T(8,128)(2,1)S(1)}, bf16[1,8,512]{2,1,0:T(8,128)(2,1)}, u32[]{:S(2)}) %copy-start.2) | copy-done | bytes 8216
  3.6 0.0 copy-start.3
  3.6 0.7 %copy-done.3 = s32[32]{0:T(128)S(1)} copy-done((s32[32]{0:T(128)S(1)}, s32[32]{0:T(128)}, u32[]{:S(2)}) %copy-start.3) | copy-done | bytes 152
  4.3 0.0 copy-start.4
  4.3 0.7 %copy-done.4 = s32[32]{0:T(128)S(1)} copy-done((s32[32]{0:T(128)S(1)}, s32[32]{0:T(128)}, u32[]{:S(2)}) %copy-start.4) | copy-done | bytes 152
  5.0 0.0 copy-start.5
  5.0 0.7 %copy-done.5 = f32[32]{0:T(128)S(1)} copy-done((f32[32]{0:T(128)S(1)}, f32[32]{0:T(128)}, u32[]{:S(2)}) %copy-start.5) | copy-done | bytes 152
  5.6 31.2 %shard_map.145 = (bf16[768,2048]{1,0:T(8,128)(2,1)}, f32[8,2048]{1,0:T(8,128)S(1)}, f32[8,512]{1,0:T(8,128)S(1)}, f32[32,2048]{1,0:T(8,128)S(1)}, f32[1,1]{1,0:T(1,128)}, /*index=5*/f32[1,32]{1,0:T(1,128)S(1)}) custom-call(bf16[768,2048]{1,0:T(8,128)(2,1)} %bitcast.21, bf16[768,2048]{1,0:T(8,128)(2,1)} %bitcast.22, bf16[2048,2048]{1,0:T(8,128)(2,1)} %inv_hbm.1, ...), custom_call_target="tpu_custom_call" | custom-call | tf_op jit(solution)/shard_map/pallas_call | solution.py:499
  36.8 4.0 %copy.23 = bf16[32,24,2048]{2,1,0:T(8,128)(2,1)} copy(bf16[32,24,2048]{2,1,0:T(8,128)(2,1)} %bitcast.20) | data formatting | bytes 6291456
  40.8 0.6 %copy.24 = f32[8,2048]{1,0:T(8,128)} copy(f32[8,2048]{1,0:T(8,128)S(1)} %get-tuple-element.25) | data formatting | bytes 131072
  41.4 0.6 %copy.25 = f32[1,8,512]{2,1,0:T(8,128)} copy(f32[1,8,512]{2,1,0:T(8,128)S(1)} %bitcast.14) | data formatting | bytes 32768
  42.0 0.7 %copy.26 = f32[4,8,2048]{2,1,0:T(8,128)} copy(f32[4,8,2048]{2,1,0:T(8,128)S(1)} %bitcast.12) | data formatting | bytes 524288
  43.3 0.5 %copy.28 = f32[32]{0:T(128)} copy(f32[32]{0:T(128)S(1)} %bitcast.19) | data formatting | bytes 256
Async XLA Ops:
  1.3 0.9 %copy-start = (bf16[4,8,2048]{2,1,0:T(8,128)(2,1)S(1)}, bf16[4,8,2048]{2,1,0:T(8,128)(2,1)}, u32[]{:S(2)}) copy-start(bf16[4,8,2048]{2,1,0:T(8,128)(2,1)} %param.17) | copy-start | bytes 393220
  2.2 0.8 %copy-start.1 = (bf16[8,2048]{1,0:T(8,128)(2,1)S(1)}, bf16[8,2048]{1,0:T(8,128)(2,1)}, u32[]{:S(2)}) copy-start(bf16[8,2048]{1,0:T(8,128)(2,1)} %pf_ref.1) | copy-start | bytes 98308
  2.9 0.7 %copy-start.2 = (bf16[1,8,512]{2,1,0:T(8,128)(2,1)S(1)}, bf16[1,8,512]{2,1,0:T(8,128)(2,1)}, u32[]{:S(2)}) copy-start(bf16[1,8,512]{2,1,0:T(8,128)(2,1)} %param.16) | copy-start | bytes 24580
  3.6 0.7 %copy-start.3 = (s32[32]{0:T(128)S(1)}, s32[32]{0:T(128)}, u32[]{:S(2)}) copy-start(s32[32]{0:T(128)} %b_smem.1) | copy-start | bytes 388
  4.3 0.7 %copy-start.4 = (s32[32]{0:T(128)S(1)}, s32[32]{0:T(128)}, u32[]{:S(2)}) copy-start(s32[32]{0:T(128)} %param.13) | copy-start | bytes 388
  5.0 0.7 %copy-start.5 = (f32[32]{0:T(128)S(1)}, f32[32]{0:T(128)}, u32[]{:S(2)}) copy-start(f32[32]{0:T(128)} %param.19) | copy-start | bytes 388

commit v2 on v1

--- a/solution.py
+++ b/solution.py
@@ -22,16 +22,16 @@
     c_hbm,
     d_hbm,
     inv_hbm,
-    w_ref,
-    b_ref,
+    w_hbm,
+    b_hbm,
     b_smem,
-    pf_ref,
-    ps_ref,
+    pf_hbm,
+    ps_hbm,
     pt_hbm,
     em_ref,
-    ed_ref,
-    duals_ref,
-    first_ref,
+    ed_hbm,
+    x_ref,
+    avg_ref,
     second_ref,
     third_ref,
     level_ref,
@@ -40,11 +40,9 @@
     d_ref,
     inv_ref,
     t_ref,
-    x_ref,
     s_ref,
     w_mat,
     tab_ref,
-    avg_ref,
     tl_ref,
     pt_tab,
     sec_tab,
@@ -58,7 +56,13 @@
     fs_recv,
     z_ref,
     cost_ref,
+    w_ref,
+    b_ref,
+    pf_ref,
+    ps_ref,
+    ed_ref,
     load_sem,
+    small_sem,
     meta_ssem,
     meta_rsem,
     eta_ssem,
@@ -119,6 +123,18 @@
             src.at[:, chunk(k)], dst.at[:, chunk(k)], load_sem.at[which, k]
         )
 
+    def fetch(k):
+        src, dst = (
+            (w_hbm, w_ref),
+            (b_hbm, b_ref),
+            (ps_hbm, ps_ref),
+            (pf_hbm, pf_ref),
+            (ed_hbm, ed_ref),
+        )[k]
+        return pltpu.make_async_copy(src, dst, small_sem.at[k])
+
+    for k in range(5):
+        fetch(k).start()
     for k in range(CHUNKS):
         load(k, 0).start()
         load(k, 1).start()
@@ -135,6 +151,8 @@
             barrier, inc=1, device_id={"node": lax.rem(me + r, n)}, device_id_type=MESH
         )
 
+    for k in range(5):
+        fetch(k).wait()
     weight_row = w_ref[...].astype(F32)
     branch_row = lax.rem(b_ref[...], BRANCH).astype(F32)
     meta_ref[me] = jnp.zeros(meta_ref.shape[1:], F32)
@@ -219,7 +237,7 @@
         x1_send[k] = s_ref[peer_rows, chunk(k)].astype(BF16)
         x1_copy(k).start()
     for j in range(4):
-        fs_send[j] = s_ref[0 : 2 * hs, j * quart : (j + 1) * quart].astype(BF16)
+        fs_send[j] = s_ref[0 : 2 * hs, j * quart : (j + 1) * quart]
 
     def fs_copy(r):
         to = lax.rem(quarter + r, 4)
@@ -243,7 +261,7 @@
     pair = s_ref[0 : 2 * hs, my_cols]
     for r in range(1, 4):
         fs_copy(r).wait_recv()
-        pair = pair + fs_recv[r].astype(F32)
+        pair = pair + fs_recv[r]
     z_ref[team] = pair[0:hs]
 
     def z_copy(r):
@@ -415,31 +433,6 @@
             tl_ref[...], inv_ref[:, part], preferred_element_type=F32
         ).reshape(avg_ref.shape[0], hs, tile)
 
-    @pl.loop(0, scen // 2)
-    def _(i):
-        window = pl.ds(pl.multiple_of(i * 2 * hours, 16), 2 * hours)
-        b0 = lax.rem(b_smem[2 * i], BRANCH)
-        b1 = lax.rem(b_smem[2 * i + 1], BRANCH)
-        for k in range(CHUNKS):
-            first = avg_ref[0, :, chunk(k)]
-            second = avg_ref[1, :, chunk(k)]
-            mean = jnp.concatenate(
-                (
-                    first,
-                    second,
-                    avg_ref[2 + b0, :, chunk(k)],
-                    first,
-                    second,
-                    avg_ref[2 + b1, :, chunk(k)],
-                ),
-                axis=0,
-            )
-            duals_ref[window, chunk(k)] = (
-                d_ref[window, chunk(k)].astype(F32)
-                + PENALTY * (x_ref[window, chunk(k)] - mean)
-            ).astype(BF16)
-
-    first_ref[...] = avg_ref[0]
     second_ref[...] = avg_ref[1, :, my_cols]
     third_ref[...] = avg_ref[pl.ds(2 + 4 * quarter, 4)].reshape(4 * hs, cols)
 
@@ -471,6 +464,65 @@
         x1_copy(k).wait_send()
         x2_copy(k).wait_send()
         x3_copy(k).wait_send()
+
+
+def finish(
+    b_smem,
+    x_ref,
+    d_ref,
+    avg_ref,
+    second_in,
+    third_in,
+    level_in,
+    ednew_in,
+    duals_ref,
+    first_ref,
+    second_ref,
+    third_ref,
+    level_ref,
+    ednew_ref,
+):
+    step = pl.program_id(0)
+    cols = x_ref.shape[1]
+    hours = 3 * avg_ref.shape[1]
+    pairs = x_ref.shape[0] // (2 * hours)
+    width = cols // CHUNKS
+
+    @pl.when(step == 0)
+    def _():
+        first_ref[...] = avg_ref[0]
+        second_ref[...] = second_in[...]
+        third_ref[...] = third_in[...]
+        level_ref[...] = level_in[...]
+        ednew_ref[...] = ednew_in[...]
+
+    for i in range(pairs):
+        window = slice(i * 2 * hours, (i + 1) * 2 * hours)
+        b0 = lax.rem(b_smem[2 * (step * pairs + i)], BRANCH)
+        b1 = lax.rem(b_smem[2 * (step * pairs + i) + 1], BRANCH)
+        for k in range(CHUNKS):
+            part = slice(k * width, (k + 1) * width)
+            first = avg_ref[0, :, part]
+            second = avg_ref[1, :, part]
+            mean = jnp.concatenate(
+                (
+                    first,
+                    second,
+                    avg_ref[2 + b0, :, part],
+                    first,
+                    second,
+                    avg_ref[2 + b1, :, part],
+                ),
+                axis=0,
+            )
+            duals_ref[window, part] = (
+                d_ref[window, part].astype(F32)
+                + PENALTY * (x_ref[window, part] - mean)
+            ).astype(BF16)
+
+
+def stay(value):
+    return pltpu.with_memory_space_constraint(value, pltpu.HBM)
 
 
 def body(
@@ -494,30 +546,30 @@
     half = BRANCH * hs // 2
     vmem = pl.BlockSpec(memory_space=pltpu.VMEM)
     smem = pl.BlockSpec(memory_space=pltpu.SMEM)
-    anywhere = pl.BlockSpec(memory_space=pl.ANY)
+    hbm = pl.BlockSpec(memory_space=pltpu.HBM)
     dma = pltpu.SemaphoreType.DMA
     outs = pl.pallas_call(
         functools.partial(kernel, n),
         out_shape=(
-            jax.ShapeDtypeStruct((rows, cols), BF16),
-            jax.ShapeDtypeStruct((hs, cols), F32),
+            jax.ShapeDtypeStruct((rows, cols), F32),
+            jax.ShapeDtypeStruct((lines // hs, hs, cols), F32),
             jax.ShapeDtypeStruct((hs, quart), F32),
             jax.ShapeDtypeStruct((4 * hs, cols), F32),
             jax.ShapeDtypeStruct((1, 1), F32),
             jax.ShapeDtypeStruct((1, scen), F32),
         ),
         in_specs=[
-            anywhere,
-            anywhere,
-            anywhere,
-            vmem,
-            vmem,
+            hbm,
+            hbm,
+            hbm,
+            hbm,
+            hbm,
             smem,
-            vmem,
-            vmem,
-            anywhere,
+            hbm,
+            hbm,
+            hbm,
             smem,
-            vmem,
+            hbm,
         ],
         out_specs=(vmem,) * 6,
         scratch_shapes=[
@@ -525,10 +577,8 @@
             pltpu.VMEM((rows, cols), BF16),
             pltpu.VMEM((cols, cols), BF16),
             pltpu.VMEM((rows, cols), BF16),
-            pltpu.VMEM((rows, cols), F32),
             pltpu.VMEM((lines, cols + 128), F32),
             pltpu.VMEM((lines, rows), BF16),
-            pltpu.VMEM((lines // hs, hs, cols), F32),
             pltpu.VMEM((lines // hs, hs, cols), F32),
             pltpu.VMEM((lines, cols), BF16),
             pltpu.VMEM((4, 4 * hs, cols), BF16),
@@ -539,11 +589,17 @@
             pltpu.VMEM((CHUNKS, half, width), BF16),
             pltpu.VMEM((CHUNKS, half, width), BF16),
             pltpu.VMEM((CHUNKS, half, width), BF16),
-            pltpu.VMEM((4, 2 * hs, quart), BF16),
-            pltpu.VMEM((4, 2 * hs, quart), BF16),
+            pltpu.VMEM((4, 2 * hs, quart), F32),
+            pltpu.VMEM((4, 2 * hs, quart), F32),
             pltpu.VMEM((n // 4, hs, quart), F32),
             pltpu.VMEM((rows, 128), F32),
+            pltpu.VMEM((1, scen), jnp.int32),
+            pltpu.VMEM((1, scen), jnp.int32),
+            pltpu.VMEM((hs, cols), BF16),
+            pltpu.VMEM((hs, quart), BF16),
+            pltpu.VMEM((1, scen), F32),
             dma((4, CHUNKS)),
+            dma((5,)),
             dma((n,)),
             dma((n,)),
             dma((n,)),
@@ -566,22 +622,44 @@
             dma((4,)),
         ],
         compiler_params=pltpu.CompilerParams(
-            collective_id=0, has_side_effects=True, vmem_limit_bytes=52 * 2**20
+            collective_id=0, has_side_effects=True, vmem_limit_bytes=40 * 2**20
         ),
     )(
-        unit_costs.reshape(rows, cols),
-        hour_duals.reshape(rows, cols),
-        inverse,
-        weights.reshape(1, scen),
-        section_three.reshape(1, scen),
+        stay(unit_costs.reshape(rows, cols)),
+        stay(hour_duals.reshape(rows, cols)),
+        stay(inverse),
+        stay(weights.reshape(1, scen)),
+        stay(section_three.reshape(1, scen)),
         section_three,
-        prev_first,
-        prev_second.reshape(hs, quart),
-        prev_third.reshape(4 * hs, cols),
+        stay(prev_first),
+        stay(prev_second.reshape(hs, quart)),
+        stay(prev_third.reshape(4 * hs, cols)),
         eta_mean,
-        eta_duals.reshape(1, scen),
-    )
-    duals_new, first_avg, second_avg, third_avg, level, eta_new = outs
+        stay(eta_duals.reshape(1, scen)),
+    )
+    steps = max(k for k in (1, 2, 4) if scen % (2 * k) == 0)
+    block = rows // steps
+
+    def fixed(*shape):
+        return pl.BlockSpec(shape, lambda i: (0,) * len(shape))
+
+    moving = pl.BlockSpec((block, cols), lambda i: (i, 0))
+    smalls = (fixed(hs, quart), fixed(4 * hs, cols), fixed(1, 1), fixed(1, scen))
+    duals_new, first_avg, second_avg, third_avg, level, eta_new = pl.pallas_call(
+        finish,
+        grid=(steps,),
+        out_shape=(
+            jax.ShapeDtypeStruct((rows, cols), BF16),
+            jax.ShapeDtypeStruct((hs, cols), F32),
+            jax.ShapeDtypeStruct((hs, quart), F32),
+            jax.ShapeDtypeStruct((4 * hs, cols), F32),
+            jax.ShapeDtypeStruct((1, 1), F32),
+            jax.ShapeDtypeStruct((1, scen), F32),
+        ),
+        in_specs=[smem, moving, moving, fixed(lines // hs, hs, cols), *smalls],
+        out_specs=(moving, fixed(hs, cols), *smalls),
+        compiler_params=pltpu.CompilerParams(vmem_limit_bytes=24 * 2**20),
+    )(section_three, outs[0], stay(hour_duals.reshape(rows, cols)), *outs[1:])
     return (
         duals_new.reshape(scen, hours, cols),
         first_avg,

time: 45.2 us -> 39.7 us (0.88)
  local copies, waits for them, and re-layouts: 10.7 us -> 0.01 us
  Pallas kernels: 31.2 us -> 37.9 us
  between operations: 3 us -> 1.3 us
    unnamed x17 -> x2, local copies, waits for them, and re-layouts: 10.7 us -> 0.01 us
    pallas_call x0 -> x1, Pallas kernels: none -> 5.18 us  [body(): pl.pallas_call(finish, grid=(steps,), out_shape=(jax.ShapeDtypeStruct((ro...]
    pallas_call x1, Pallas kernels: 31.2 us -> 32.7 us  [body(): pl.pallas_call(functools.partial(kernel, n), out_shape=(jax.ShapeDtypeStr...]
where the time goes in v2:
time: 39.7 us; the launch traced here: 39.2 us
  Pallas kernels  37.9 us (95%)
  between operations  1.3 us (3%)
    pallas_call x1, Pallas kernels, body(): pl.pallas_call(functools.partial(kernel, n), out_shape=(jax.ShapeDtypeStr...  32.7 us
    pallas_call x1, Pallas kernels, body(): pl.pallas_call(finish, grid=(steps,), out_shape=(jax.ShapeDtypeStruct((ro...  5.18 us

profile of v2, /device:TPU:0, one launch (start us, length us, event | category | flops | bytes accessed | tf_op | source)
XLA Modules:
  0.0 39.2 jit_solution(2839146669873388362)
XLA Ops:
  1.3 0.0 copy-start
  1.3 32.7 %shard_map.145 = (f32[768,2048]{1,0:T(8,128)S(1)}, f32[18,8,2048]{2,1,0:T(8,128)S(1)}, f32[8,512]{1,0:T(8,128)S(1)}, f32[32,2048]{1,0:T(8,128)S(1)}, f32[1,1]{1,0:T(1,128)}, /*index=5*/f32[1,32]{1,0:T(1,128)S(1)}) custom-call(bf16[768,2048]{1,0:T(8,128)(2,1)} %bitcast.15, bf16[768,2048]{1,0:T(8,128)(2,1)} %bitcast.13, bf16[2048,2048]{1,0:T(8,128)(2,1)} %inv_hbm.1, ...), custom_call_target="tpu_custom_call" | custom-call | tf_op jit(solution)/shard_map/pallas_call | solution.py:551
  34.0 0.0 copy-done
  34.1 5.2 %shard_map.146 = (bf16[768,2048]{1,0:T(8,128)(2,1)}, f32[8,2048]{1,0:T(8,128)}, f32[8,512]{1,0:T(8,128)}, f32[32,2048]{1,0:T(8,128)}, f32[1,1]{1,0:T(1,128)}, /*index=5*/f32[1,32]{1,0:T(1,128)}) custom-call(s32[32]{0:T(128)S(1)} %copy-done, f32[768,2048]{1,0:T(8,128)S(1)} %get-tuple-element.18.x_ref, bf16[768,2048]{1,0:T(8,128)(2,1)} %bitcast.14, ...), custom_call_target="tpu_custom_call" | custom-call | tf_op jit(solution)/shard_map/pallas_call | solution.py:648
Async XLA Ops:
  1.3 32.8 %copy-start = (s32[32]{0:T(128)S(1)}, s32[32]{0:T(128)}, u32[]{:S(2)}) copy-start(s32[32]{0:T(128)} %b_smem.3) | copy-start | bytes 388
